TPU v7x, 32 devices: a whole 2x2x4 slice. The times are simulated.
32 devices in a mesh: docs: 16 (over z, y, x), lists: 2 (over core).
Axes of the slice: x: 2, y: 2, z: 4, core: 2. Of those that a mesh axis runs over, the one named last changes fastest.
Arguments:
- tokens: float32 [2, 32, 512, 768], P('lists', 'docs'), may hold values from -6 to 6
- pair_lengths: int32 [2, 32, 6], P('lists', 'docs'), may hold values from 1 to 128, 480 in all within a row
- list_ids: int32 [2, 192], P('lists'), may hold values from 0 to 7
- relevance: int32 [2, 192], P('lists'), may hold values from 0 to 3
- first_gain: float32 [768], replicated, may hold values from 0.5 to 1.5
- query_weight: float32 [768, 768], replicated, may hold values from -0.02734375 to 0.02734375
- key_weight: float32 [768, 768], replicated, may hold values from -0.21875 to 0.21875
- value_weight: float32 [768, 768], replicated, may hold values from -0.21875 to 0.21875
- output_weight: float32 [768, 768], replicated, may hold values from -0.875 to 0.875
- bias_table: float32 [32, 12], replicated, may hold values from -4 to 4
- second_gain: float32 [768], replicated, may hold values from 0.5 to 1.5
- inner_weight: float32 [768, 3072], replicated, may hold values from -0.21875 to 0.21875
- outer_weight: float32 [3072, 768], replicated, may hold values from -0.109375 to 0.109375
- final_gain: float32 [768], replicated, may hold values from 0.5 to 1.5
- score_vector: float32 [768], replicated, may hold values from -0.625 to 0.625
Outputs:
- encoded: float32 [2, 32, 512, 768], P('lists', 'docs')
- scores: float32 [2, 32, 6], P('lists', 'docs')
- tokens_grad: float32 [2, 32, 512, 768], P('lists', 'docs')
- first_gain_grad: float32 [768], replicated
- query_weight_grad: float32 [768, 768], replicated
- key_weight_grad: float32 [768, 768], replicated
- value_weight_grad: float32 [768, 768], replicated
- output_weight_grad: float32 [768, 768], replicated
- bias_table_grad: float32 [32, 12], replicated
- second_gain_grad: float32 [768], replicated
- inner_weight_grad: float32 [768, 3072], replicated
- outer_weight_grad: float32 [3072, 768], replicated
- final_gain_grad: float32 [768], replicated
- score_vector_grad: float32 [768], replicated
Inputs may be any that keep to these rules, and one draw needn't show every extreme that they name: `pair_lengths`: in every row the 6 lengths add up to 480 and the largest is exactly 128; the last 32 positions of a row are padding.
All inputs are finite; a program needn't handle non-finite values.
Results may differ from a plain program's by a relative error of at most 0.02.
Values may be sent and summed in bfloat16 or wider, within the bound.
No kernel may reach another device: no remote copies, remote signals or barrier semaphores. Data moves between devices by JAX's collectives and lax.ppermute only.
A program may use at most 256 MiB of HBM per device.

v0:
```python
import jax
import jax.numpy as jnp
from jax import lax
from jax.sharding import PartitionSpec as P

epsilon = 1e-06
negative = -1000000000.0
highest = lax.Precision.HIGHEST
limits = (12, 16, 23, 32, 46, 64, 91)


def smooth_gate(values):
    return jax.nn.gelu(values, approximate=True)


def bucket_of(offsets):
    upper_half = jnp.where(offsets > 0, 16, 0).astype(jnp.int32)
    distance = jnp.abs(offsets)
    passed = jnp.stack([(distance >= border).astype(jnp.int32) for border in limits], axis=0)
    beyond = 8 + jnp.sum(passed, axis=0, dtype=jnp.int32)
    return upper_half + jnp.where(distance < 8, distance, beyond)


def norm_scale(inputs):
    return lax.rsqrt(jnp.mean(inputs * inputs, axis=-1, keepdims=True) + epsilon)


def norm_back(normed, factor, upstream):
    return factor * (upstream - normed * jnp.mean(upstream * normed, axis=-1, keepdims=True))


def outer_sum(left_rows, right_rows):
    return jnp.einsum("rd,re->de", left_rows, right_rows, preferred_element_type=jnp.float32)


def times_transpose(left_rows, right_rows):
    return lax.dot_general(
        left_rows, right_rows, (((1,), (1,)), ((), ())), preferred_element_type=jnp.float32
    )


def shards(
    tokens,
    pair_lengths,
    list_ids,
    relevance,
    first_gain,
    query_weight,
    key_weight,
    value_weight,
    output_weight,
    bias_table,
    second_gain,
    inner_weight,
    outer_weight,
    final_gain,
    score_vector,
):
    row_count = tokens.shape[1]
    row_length = tokens.shape[2]
    model_width = tokens.shape[3]
    pair_count = pair_lengths.shape[2]
    buckets = bias_table.shape[0]
    head_count = bias_table.shape[1]
    head_size = model_width // head_count
    hidden_width = inner_weight.shape[1]
    row_pairs = row_count * pair_count
    token_rows = tokens.reshape(row_count, row_length, model_width)
    row_lengths = pair_lengths.reshape(row_count, pair_count)
    joined_weight = jnp.concatenate((query_weight, key_weight, value_weight), axis=1).astype(
        jnp.bfloat16
    )
    output_low = output_weight.astype(jnp.bfloat16)
    inner_low = inner_weight.astype(jnp.bfloat16)
    outer_low = outer_weight.astype(jnp.bfloat16)
    positions = jnp.arange(row_length, dtype=jnp.int32)
    bucket_grid = bucket_of(positions[None, :] - positions[:, None])
    bucket_onehot = (
        bucket_grid[:, :, None] == jnp.arange(buckets, dtype=jnp.int32)[None, None, :]
    ).astype(jnp.float32)
    position_bias = jnp.einsum("qkb,bh->hqk", bucket_onehot, bias_table, precision=highest)

    def split_heads(projected, column, rows_taken):
        return projected[:, column * model_width : (column + 1) * model_width].reshape(
            rows_taken, head_count, head_size
        )

    def forward_row(row_item):
        token_row, lengths = row_item
        pair_ends = jnp.cumsum(lengths, dtype=jnp.int32)
        starts = pair_ends - lengths
        segment = jnp.sum(
            (positions[:, None] >= pair_ends[None, :]).astype(jnp.int32), axis=1, dtype=jnp.int32
        )
        allowed = segment[:, None] == segment[None, :]
        normed_one = (token_row * norm_scale(token_row) * first_gain).astype(jnp.bfloat16)
        projected = jnp.dot(normed_one, joined_weight, preferred_element_type=jnp.float32).astype(
            jnp.bfloat16
        )
        queries = split_heads(projected, 0, row_length)
        key_rows = split_heads(projected, 1, row_length)
        value_rows = split_heads(projected, 2, row_length)
        logits = (
            jnp.einsum("qhd,khd->hqk", queries, key_rows, preferred_element_type=jnp.float32)
            + position_bias
        )
        logits = jnp.where(allowed[None], logits, negative)
        row_peak = jnp.max(logits, axis=-1, keepdims=True)
        log_total = row_peak + jnp.log(jnp.sum(jnp.exp(logits - row_peak), axis=-1, keepdims=True))
        probs_low = jnp.exp(logits - log_total).astype(jnp.bfloat16)
        context = jnp.einsum(
            "hqk,khd->qhd", probs_low, value_rows, preferred_element_type=jnp.float32
        )
        context = context.reshape(row_length, model_width).astype(jnp.bfloat16)
        attended = token_row + jnp.dot(context, output_low, preferred_element_type=jnp.float32)
        normed_two = (attended * norm_scale(attended) * second_gain).astype(jnp.bfloat16)
        preact = jnp.dot(normed_two, inner_low, preferred_element_type=jnp.float32)
        hidden = smooth_gate(preact).astype(jnp.bfloat16)
        encoded_row = attended + jnp.dot(hidden, outer_low, preferred_element_type=jnp.float32)
        first_out = encoded_row[starts]
        final_normed = first_out * norm_scale(first_out)
        row_scores = jnp.dot(final_normed * final_gain, score_vector, precision=highest)
        kept_row = (
            starts,
            segment,
            projected,
            log_total[:, starts, :],
            context[starts],
            attended[starts],
            normed_two[starts],
            preact[starts],
            hidden[starts],
            first_out,
        )
        return (encoded_row, row_scores, kept_row)

    encoded_rows, pair_scores, kept_rows = lax.map(forward_row, (token_rows, row_lengths))
    flat_scores = pair_scores.reshape(row_pairs)
    docs_index = lax.axis_index("docs")
    group_ids = list_ids.reshape(-1)
    group_labels = relevance.reshape(-1).astype(jnp.float32)
    list_count = lax.axis_size("docs") // 2
    list_range = jnp.arange(list_count, dtype=jnp.int32)
    group_member = group_ids[:, None] == list_range[None, :]
    label_totals = jnp.sum(jnp.where(group_member, group_labels[:, None], 0.0), axis=0)
    own_ids = lax.dynamic_slice_in_dim(group_ids, docs_index * row_pairs, row_pairs)
    own_labels = lax.dynamic_slice_in_dim(group_labels, docs_index * row_pairs, row_pairs)
    own_member = own_ids[:, None] == list_range[None, :]
    all_scores = lax.all_gather(flat_scores, "docs", axis=0, tiled=True)
    list_top = jnp.max(jnp.where(group_member, all_scores[:, None], negative), axis=0)
    list_total = jnp.sum(
        jnp.exp(jnp.where(group_member, all_scores[:, None] - list_top[None, :], negative)), axis=0
    )
    pair_top = jnp.sum(jnp.where(own_member, list_top[None, :], 0.0), axis=1)
    pair_total = jnp.sum(jnp.where(own_member, list_total[None, :], 0.0), axis=1)
    pair_labels = jnp.sum(jnp.where(own_member, label_totals[None, :], 0.0), axis=1)
    pair_grad = jnp.exp(flat_scores - pair_top) / pair_total * pair_labels - own_labels

    def backward_row(totals, row_item):
        token_row, row_grad, kept_row = row_item
        (
            starts,
            segment,
            projected,
            log_first,
            context_first,
            attended_first,
            normed_two_first,
            preact_first,
            hidden_first,
            first_out,
        ) = kept_row
        scale_final = norm_scale(first_out)
        final_normed = first_out * scale_final
        grad_final = row_grad[:, None] * score_vector[None, :]
        grad_encoded = norm_back(final_normed, scale_final, grad_final * final_gain)
        grad_branch = grad_encoded.astype(jnp.bfloat16)
        grad_hidden = times_transpose(grad_branch, outer_low)
        gate_value, gate_pull = jax.vjp(smooth_gate, preact_first)
        grad_preact = gate_pull(grad_hidden)[0].astype(jnp.bfloat16)
        grad_normed_two = times_transpose(grad_preact, inner_low)
        scale_two = norm_scale(attended_first)
        second_normed = attended_first * scale_two
        grad_attended = grad_encoded + norm_back(
            second_normed, scale_two, grad_normed_two * second_gain
        )
        grad_attn = grad_attended.astype(jnp.bfloat16)
        grad_context = times_transpose(grad_attn, output_low).astype(jnp.bfloat16)
        grad_context = grad_context.reshape(pair_count, head_count, head_size)
        query_first = split_heads(projected[starts], 0, pair_count)
        key_rows = split_heads(projected, 1, row_length)
        value_rows = split_heads(projected, 2, row_length)
        allowed_first = segment[starts][:, None] == segment[None, :]
        logits = jnp.einsum(
            "phd,khd->hpk", query_first, key_rows, preferred_element_type=jnp.float32
        )
        logits = jnp.where(allowed_first[None], logits + position_bias[:, starts, :], negative)
        probs = jnp.exp(logits - log_first)
        grad_probs = jnp.einsum(
            "phd,khd->hpk", grad_context, value_rows, preferred_element_type=jnp.float32
        )
        grad_logits = (
            probs * (grad_probs - jnp.sum(probs * grad_probs, axis=-1, keepdims=True))
        ).astype(jnp.bfloat16)
        grad_table = jnp.einsum(
            "hpk,pkb->bh", grad_logits.astype(jnp.float32), bucket_onehot[starts], precision=highest
        )
        grad_queries = jnp.einsum(
            "hpk,khd->phd", grad_logits, key_rows, preferred_element_type=jnp.float32
        )
        grad_queries = grad_queries.reshape(pair_count, model_width).astype(jnp.bfloat16)
        grad_keys = jnp.einsum(
            "hpk,phd->khd", grad_logits, query_first, preferred_element_type=jnp.float32
        )
        grad_keys = grad_keys.reshape(row_length, model_width).astype(jnp.bfloat16)
        grad_values = jnp.einsum(
            "hpk,phd->khd",
            probs.astype(jnp.bfloat16),
            grad_context,
            preferred_element_type=jnp.float32,
        )
        grad_values = grad_values.reshape(row_length, model_width).astype(jnp.bfloat16)
        scale_one = norm_scale(token_row)
        first_normed = token_row * scale_one
        normed_one = (first_normed * first_gain).astype(jnp.bfloat16)
        grad_normed_one = times_transpose(
            jnp.concatenate((grad_keys, grad_values), axis=1), joined_weight[:, model_width:]
        )
        grad_normed_one = grad_normed_one.at[starts].add(
            times_transpose(grad_queries, joined_weight[:, :model_width])
        )
        grad_row = (
            norm_back(first_normed, scale_one, grad_normed_one * first_gain)
            .at[starts]
            .add(grad_attended)
        )
        totals = (
            totals[0] + outer_sum(normed_one, grad_keys),
            totals[1] + outer_sum(normed_one, grad_values),
            totals[2] + grad_table,
            totals[3] + jnp.sum(first_normed * grad_normed_one, axis=0),
            totals[4] + jnp.sum(second_normed * grad_normed_two, axis=0),
            totals[5] + jnp.sum(final_normed * grad_final, axis=0),
            totals[6] + jnp.sum(final_normed * final_gain * row_grad[:, None], axis=0),
        )
        rows_out = (
            normed_one[starts],
            grad_queries,
            context_first,
            grad_attn,
            normed_two_first,
            grad_preact,
            hidden_first,
            grad_branch,
        )
        return (totals, (grad_row, rows_out))

    zeros_square = jnp.zeros((model_width, model_width), jnp.float32)
    zeros_vector = jnp.zeros((model_width,), jnp.float32)
    initial = (
        zeros_square,
        zeros_square,
        jnp.zeros((buckets, head_count), jnp.float32),
        zeros_vector,
        zeros_vector,
        zeros_vector,
        zeros_vector,
    )
    totals, (grad_rows, pair_rows) = lax.scan(
        backward_row, initial, (token_rows, pair_grad.reshape(row_count, pair_count), kept_rows)
    )
    (
        normed_first,
        grad_queries,
        context_first,
        grad_attn,
        normed_two_first,
        grad_preact,
        hidden_first,
        grad_branch,
    ) = tuple((member.reshape(row_pairs, member.shape[-1]) for member in pair_rows))
    (
        grad_key_weight,
        grad_value_weight,
        grad_table,
        grad_first,
        grad_second,
        grad_final,
        grad_vector,
    ) = totals
    term_query = outer_sum(normed_first, grad_queries)
    term_output = outer_sum(context_first, grad_attn)
    term_inner = outer_sum(normed_two_first, grad_preact)
    term_outer = outer_sum(hidden_first, grad_branch)
    shares = (
        lax.psum_scatter(
            term_query.reshape(-1), ("docs", "lists"), scatter_dimension=0, tiled=True
        ),
        lax.psum_scatter(
            grad_key_weight.reshape(-1), ("docs", "lists"), scatter_dimension=0, tiled=True
        ),
        lax.psum_scatter(
            grad_value_weight.reshape(-1), ("docs", "lists"), scatter_dimension=0, tiled=True
        ),
        lax.psum_scatter(
            term_output.reshape(-1), ("docs", "lists"), scatter_dimension=0, tiled=True
        ),
        lax.psum_scatter(
            term_inner.reshape(-1), ("docs", "lists"), scatter_dimension=0, tiled=True
        ),
        lax.psum_scatter(
            term_outer.reshape(-1), ("docs", "lists"), scatter_dimension=0, tiled=True
        ),
    )
    gathered = (
        lax.all_gather(
            shares[0].astype(jnp.bfloat16), ("docs", "lists"), axis=0, tiled=True
        ).astype(jnp.float32),
        lax.all_gather(
            shares[1].astype(jnp.bfloat16), ("docs", "lists"), axis=0, tiled=True
        ).astype(jnp.float32),
        lax.all_gather(
            shares[2].astype(jnp.bfloat16), ("docs", "lists"), axis=0, tiled=True
        ).astype(jnp.float32),
        lax.all_gather(
            shares[3].astype(jnp.bfloat16), ("docs", "lists"), axis=0, tiled=True
        ).astype(jnp.float32),
        lax.all_gather(
            shares[4].astype(jnp.bfloat16), ("docs", "lists"), axis=0, tiled=True
        ).astype(jnp.float32),
        lax.all_gather(
            shares[5].astype(jnp.bfloat16), ("docs", "lists"), axis=0, tiled=True
        ).astype(jnp.float32),
    )
    query_grad = gathered[0].reshape(model_width, model_width)
    key_grad = gathered[1].reshape(model_width, model_width)
    value_grad = gathered[2].reshape(model_width, model_width)
    output_grad = gathered[3].reshape(model_width, model_width)
    inner_grad = gathered[4].reshape(model_width, hidden_width)
    outer_grad = gathered[5].reshape(hidden_width, model_width)
    small_sums = lax.psum(
        (grad_table, grad_first, grad_second, grad_final, grad_vector), ("docs", "lists")
    )
    return (
        encoded_rows.reshape(tokens.shape),
        pair_scores.reshape(1, row_count, pair_count),
        grad_rows.reshape(tokens.shape),
        small_sums[1],
        query_grad,
        key_grad,
        value_grad,
        output_grad,
        small_sums[0],
        small_sums[2],
        inner_grad,
        outer_grad,
        small_sums[3],
        small_sums[4],
    )


def solution(mesh):
    return jax.shard_map(
        shards,
        mesh=mesh,
        in_specs=(
            P("lists", "docs", None, None),
            P("lists", "docs", None),
            P("lists", None),
            P("lists", None),
            P(),
            P(),
            P(),
            P(),
            P(),
            P(),
            P(),
            P(),
            P(),
            P(),
            P(),
        ),
        out_specs=(
            P("lists", "docs", None, None),
            P("lists", "docs", None),
            P("lists", "docs", None, None),
            P(),
            P(),
            P(),
            P(),
            P(),
            P(),
            P(),
            P(),
            P(),
            P(),
            P(),
        ),
        check_vma=False,
    )
```

profile of v0, /device:TPU:0, one launch (start us, length us, event | category | flops | bytes accessed | tf_op | source)
XLA Modules:
  0.0 1325.4 jit_solution(12363276916353542197)
XLA Ops:
  27.5 13.6 %fusion.87 = f32[12,512,512]{2,0,1:T(8,128)} fusion(s32[512,512]{1,0:T(8,128)S(1)} %fusion.88, f32[32,12]{0,1:T(8,128)S(1)} %copy-done), kind=kOutput, calls=%fused_computation.181 | convolution fusion | flops 1216348160 | bytes 13633024 | tf_op jit(solution)/shard_map/qkb,bh->hqk/dot_general | solution.py:81
  41.2 17.7 %copy.120 = f32[12,512,512]{1,2,0:T(8,128)} copy(f32[12,512,512]{2,0,1:T(8,128)} %fusion.87) | data formatting | bytes 25165824
  65.0 154.2 %while.72 = (s32[]{:T(128)}, f32[2,512,768]{2,1,0:T(8,128)}, f32[2,6]{1,0:T(2,128)}, s32[2,6]{1,0:T(2,128)}, s32[2,512]{1,0:T(2,128)}, /*index=5*/bf16[2,512,230...) while((s32[]{:T(128)}, f32[2,512,768]{2,1,0:T(8,128)}, ...), condition=%wide.wide.region_8.9_spmd.clone, body=%wide.wide.region_0.8_spmd.clone.sunk | while | flops 8095871488 | bytes 115909184 | solution.py:137
  82.3 7.2 fusion.259
  109.7 10.0 fusion.261
  126.1 8.0 bitcast_dynamic-update-slice_fusion.36
  154.8 7.2 fusion.259
  182.2 10.0 fusion.261
  198.6 8.0 bitcast_dynamic-update-slice_fusion.36
  222.2 43.5 %all-reduce = f32[192]{0:T(256)S(1)} all-reduce(f32[192]{0:T(256)S(1)} %dynamic-update-slice), channel_id=1, replica_groups=mesh['docs'=16,'lists'=2] {'docs'}, use_global_device_ids=true, to_apply=%add | all-reduce | flops 192 | bytes 1536
  274.0 183.3 %while.71 = (s32[]{:T(128)}, f32[768,768]{1,0:T(8,128)}, f32[768,768]{1,0:T(8,128)}, f32[32,12]{0,1:T(8,128)}, f32[768]{0:T(1024)}, /*index=5*/f32[768]{0:T(1024...) while((s32[]{:T(128)}, f32[768,768]{1,0:T(8,128)}, ...), condition=%wide.region_29.30_spmd.clone, body=%wide.region_15.29_spmd.clone.sunk | while | flops 2556721408 | bytes 183615024 | solution.py:269
  292.4 7.0 gather_fusion
  349.6 11.3 fusion.239
  442.1 11.3 fusion.239
  473.1 10.7 reshape.736
  492.2 461.0 %all-reduce.9 = (f32[768]{0:T(1024)}, bf16[589824]{0:T(1024)(128)(2,1)S(1)}, bf16[589824]{0:T(1024)(128)(2,1)}, bf16[589824]{0:T(1024)(128)(2,1)}, bf16[589824]{...) all-reduce(f32[768]{0:T(1024)S(1)} %copy-done.38, ...), channel_id=1, replica_groups=mesh['docs'=16,'lists'=2] {'docs','lists'}, use_global_device_ids=true, to_apply=%region_30.31 | all-reduce | flops 7081344 | bytes 42494976 | tf_op jit(solution)/shard_map/psum | solution.py:341
  961.5 46.2 %all-gather.11.cloned.1.call-done = bf16[589824]{0:T(1024)(128)(2,1)} async-done(((bf16[18432]{0:T(1024)(128)(2,1)}), bf16[589824]{0:T(1024)(128)(2,1)}) %all-gather.11.cloned.1.call-update) | async-done | bytes 1179664 | tf_op jit(solution)/shard_map/all_gather | solution.py:322
  1011.1 53.1 %all-gather.13.cloned.1.call-done = bf16[589824]{0:T(1024)(128)(2,1)} async-done(((bf16[18432]{0:T(1024)(128)(2,1)}), bf16[589824]{0:T(1024)(128)(2,1)}) %all-gather.13.cloned.1.call-update) | async-done | bytes 1179664 | tf_op jit(solution)/shard_map/all_gather | solution.py:325
  1067.5 53.1 %all-gather.9.cloned.1.call-done = bf16[589824]{0:T(1024)(128)(2,1)} async-done(((bf16[18432]{0:T(1024)(128)(2,1)}), bf16[589824]{0:T(1024)(128)(2,1)}) %all-gather.9.cloned.1.call-update) | async-done | bytes 1179664 | tf_op jit(solution)/shard_map/all_gather | solution.py:319
  1124.0 53.0 %all-gather.7.cloned.1.call-done = bf16[589824]{0:T(1024)(128)(2,1)} async-done(((bf16[18432]{0:T(1024)(128)(2,1)}), bf16[589824]{0:T(1024)(128)(2,1)}) %all-gather.7.cloned.1.call-update) | async-done | bytes 1179664 | tf_op jit(solution)/shard_map/all_gather | solution.py:316
  1180.3 62.6 %all-gather.15.cloned.1.call-done = bf16[2359296]{0:T(1024)(128)(2,1)} async-done(((bf16[73728]{0:T(1024)(128)(2,1)}), bf16[2359296]{0:T(1024)(128)(2,1)}) %all-gather.15.cloned.1.call-update) | async-done | bytes 4718608 | tf_op jit(solution)/shard_map/all_gather | solution.py:328
  1242.9 8.7 reshape.748
  1251.7 56.5 %all-gather.17.cloned.1.call-done = bf16[2359296]{0:T(1024)(128)(2,1)} async-done(((bf16[73728]{0:T(1024)(128)(2,1)}), bf16[2359296]{0:T(1024)(128)(2,1)}) %all-gather.17.cloned.1.call-update) | async-done | bytes 4718608 | tf_op jit(solution)/shard_map/all_gather | solution.py:331
  1308.2 10.0 reshape.750
  (457 shorter events, 329.5 us)
Async XLA Ops:
  7.2 20.4 %copy-start = (f32[32,12]{0,1:T(8,128)S(1)}, f32[32,12]{0,1:T(8,128)}, u32[]{:S(2)}) copy-start(f32[32,12]{0,1:T(8,128)} %param.28) | copy-start | bytes 4612
  7.2 1000.5 %all-gather.11.cloned.1.call-start = ((), (), s32[]{:S(2)}) async-start(), calls=%async_computation.2 | async-start | bytes 1216512 | tf_op jit(solution)/shard_map/all_gather | solution.py:322
  7.8 19.7 %copy-start.16 = (s32[512,512]{1,0:T(8,128)}, s32[512,512]{1,0:T(8,128)S(1)}, u32[]{:S(2)}) copy-start(s32[512,512]{1,0:T(8,128)S(1)} %fusion.88) | copy-start | bytes 3145732
  109.7 10.1 copy-start.40
  126.0 10.2 copy-start.52
  126.0 10.4 copy-start.53
  126.1 11.7 copy-start.51
  198.5 10.2 copy-start.52
  198.6 10.4 copy-start.53
  198.6 11.7 copy-start.51
  219.2 54.8 %copy-start.31 = (bf16[2,6,3072]{2,1,0:T(8,128)(2,1)}, bf16[2,6,3072]{2,1,0:T(8,128)(2,1)S(1)}, u32[]{:S(2)}) copy-start(bf16[2,6,3072]{2,1,0:T(8,128)(2,1)S(1)} %get-tuple-element.1831) | copy-start | bytes 221188
  219.2 54.8 %copy-start.27 = (f32[768]{0:T(1024)S(1)}, f32[768]{0:T(1024)}, u32[]{:S(2)}) copy-start(f32[768]{0:T(1024)} %get-tuple-element.1843) | copy-start | bytes 9220
  275.2 11.7 copy-start.42
  277.6 25.1 %copy-start.35 = (s32[1024]{0:T(1024)}, s32[1024]{0:T(1024)S(1)}, u32[]{:S(2)}) copy-start(s32[1024]{0:T(1024)S(1)} %pad_clamp_fusion.5) | copy-start | bytes 12292 | tf_op jit(solution)/shard_map/while
  292.4 17.7 %copy-start.24 = (bf16[6,12,64]{2,1,0:T(8,128)(2,1)}, bf16[6,12,64]{2,1,0:T(8,128)(2,1)S(1)}, u32[]{:S(2)}) copy-start(bf16[6,12,64]{2,1,0:T(8,128)(2,1)S(1)} %reshape.979) | copy-start | bytes 27652 | tf_op jit(solution)/shard_map/while
  365.7 13.1 copy-start.42
  368.1 27.1 %copy-start.35 = (s32[1024]{0:T(1024)}, s32[1024]{0:T(1024)S(1)}, u32[]{:S(2)}) copy-start(s32[1024]{0:T(1024)S(1)} %pad_clamp_fusion.5) | copy-start | bytes 12292 | tf_op jit(solution)/shard_map/while
  385.0 17.7 %copy-start.24 = (bf16[6,12,64]{2,1,0:T(8,128)(2,1)}, bf16[6,12,64]{2,1,0:T(8,128)(2,1)S(1)}, u32[]{:S(2)}) copy-start(bf16[6,12,64]{2,1,0:T(8,128)(2,1)S(1)} %reshape.979) | copy-start | bytes 27652 | tf_op jit(solution)/shard_map/while
  473.1 10.7 copy-start.41
  954.5 109.7 %all-gather.13.cloned.1.call-start = ((), (), s32[]{:S(2)}) async-start(), calls=%async_computation.3 | async-start | bytes 1216512 | tf_op jit(solution)/shard_map/all_gather | solution.py:325
  956.0 164.7 %all-gather.9.cloned.1.call-start = ((), (), s32[]{:S(2)}) async-start(), calls=%async_computation.1 | async-start | bytes 1216512 | tf_op jit(solution)/shard_map/all_gather | solution.py:319
  957.5 219.5 %all-gather.7.cloned.1.call-start = ((), (), s32[]{:S(2)}) async-start(), calls=%async_computation | async-start | bytes 1216512 | tf_op jit(solution)/shard_map/all_gather | solution.py:316
  958.2 284.8 %all-gather.15.cloned.1.call-start = ((), (), s32[]{:S(2)}) async-start(), calls=%async_computation.4 | async-start | bytes 4866048 | tf_op jit(solution)/shard_map/all_gather | solution.py:328
  959.8 348.3 %all-gather.17.cloned.1.call-start = ((), (), s32[]{:S(2)}) async-start(), calls=%async_computation.5 | async-start | bytes 4866048 | tf_op jit(solution)/shard_map/all_gather | solution.py:331
  (76 other events, 280.6 us)
Sparse Core Ops, SparseCore 0:
  954.6 53.0 all-gather.10
  1011.2 52.9 all-gather.12
  1067.7 52.9 all-gather.8
  1124.0 52.9 all-gather.6
  1180.3 62.5 all-gather.14
  1245.7 62.4 all-gather.16
where the time goes:
time: 1340 us; the launch traced here: 1330 us
  blocking collectives  504 us (38%)
  waiting for transfers between devices  325 us (24%)
  local copies, waits for them, and re-layouts  228 us (17%)
  matrix products  149 us (11%)
  other arithmetic  93.9 us (7%)
  between operations  15.5 us (1%)
    psum x1, blocking collectives, shards(): lax.psum((grad_table, grad_first, grad_second, grad_final, grad_vector),...  461 us
    all_gather x1, waiting for transfers between devices, shards(): lax.all_gather(shares[4].astype(jnp.bfloat16), ('docs', 'lists'), axis=0,...  62.6 us
    all_gather x1, waiting for transfers between devices, shards(): lax.all_gather(shares[5].astype(jnp.bfloat16), ('docs', 'lists'), axis=0,...  56.5 us
    all_gather x1, waiting for transfers between devices, shards(): lax.all_gather(shares[1].astype(jnp.bfloat16), ('docs', 'lists'), axis=0,...  53.1 us
    all_gather x1, waiting for transfers between devices, shards(): lax.all_gather(shares[3].astype(jnp.bfloat16), ('docs', 'lists'), axis=0,...  53.1 us
    all_gather x1, waiting for transfers between devices, shards(): lax.all_gather(shares[0].astype(jnp.bfloat16), ('docs', 'lists'), axis=0,...  53 us
    all_gather x1, waiting for transfers between devices, shards(): lax.all_gather(shares[2].astype(jnp.bfloat16), ('docs', 'lists'), axis=0,...  46.2 us
    unnamed x1, blocking collectives  43.5 us
  transfers between devices with their start and end apart: 6, of which 6 were waited for; matrix products, arithmetic and copies ran while one was open for 2% of the time, Pallas kernels for 0%

commit v1 on v0

v1 whole, which is shorter than its diff:
```python
import functools
import math

import jax
import jax.numpy as jnp
from jax import lax
from jax.experimental import pallas as pl
from jax.experimental.pallas import tpu as pltpu
from jax.sharding import PartitionSpec as P

epsilon = 1e-06
negative = -1000000000.0
highest = lax.Precision.HIGHEST
limits = (12, 16, 23, 32, 46, 64, 91)
f32 = jnp.float32
bf16 = jnp.bfloat16
window = 128
reach = 144
lanes_path = 256
group = 16
curve = math.sqrt(2.0 / math.pi)
cubic = 0.044715
whole = pl.BlockSpec(memory_space=pltpu.VMEM)
scalars = pl.BlockSpec(memory_space=pltpu.SMEM)
anywhere = pl.BlockSpec(memory_space=pl.ANY)


def mm(a, b):
    return lax.dot_general(a, b, (((1,), (0,)), ((), ())), preferred_element_type=f32)


def mm_nt(a, b):
    return lax.dot_general(a, b, (((1,), (1,)), ((), ())), preferred_element_type=f32)


def mm_tn(a, b):
    return lax.dot_general(a, b, (((0,), (0,)), ((), ())), preferred_element_type=f32)


def iota(shape, axis):
    return lax.broadcasted_iota(jnp.int32, shape, axis)


def bucket_of(offsets):
    upper_half = jnp.where(offsets > 0, 16, 0)
    distance = jnp.abs(offsets)
    beyond = jnp.full(offsets.shape, 8, jnp.int32)
    for border in limits:
        beyond = beyond + jnp.where(distance >= border, 1, 0)
    return upper_half + jnp.where(distance < 8, distance, beyond)


def rms_factor(values):
    return lax.rsqrt(jnp.mean(values * values, axis=-1, keepdims=True) + epsilon)


def norm_back(normed, factor, upstream):
    return factor * (upstream - normed * jnp.mean(upstream * normed, axis=-1, keepdims=True))


def gelu(values):
    inner = curve * (values + cubic * (values * values * values))
    return 0.5 * values * (1.0 + jnp.tanh(inner))


def gelu_pair(values):
    square = values * values
    bent = jnp.tanh(curve * (values + cubic * (square * values)))
    half = 0.5 * (1.0 + bent)
    slope = half + 0.5 * values * (1.0 - bent * bent) * (curve * (1.0 + (3.0 * cubic) * square))
    return half * values, slope


def bias_vector(table, lanes, origin):
    buckets = table.shape[0]
    buckets_at = bucket_of(iota((buckets, lanes), 1) - origin)
    chosen = jnp.where(buckets_at == iota((buckets, lanes), 0), 1.0, 0.0)
    return lax.dot_general(
        table, chosen, (((0,), (0,)), ((), ())), precision=highest, preferred_element_type=f32
    )


def cast_rows(target, source, chunk):
    rows = source.shape[0]

    def step(i, carry):
        at = pl.ds(pl.multiple_of(i * chunk, chunk), chunk)
        target[at, :] = source[at, :].astype(bf16)
        return carry

    lax.fori_loop(0, rows // chunk, step, 0)


def starts_of(lengths, row, count):
    out, at = [], 0
    for i in range(count):
        out.append((at, lengths[row, i]))
        at = at + lengths[row, i]
    return out


def path_kernel(
    dims,
    lengths, ids, labels,
    tokens, first_gain, second_gain, final_gain, score_vector, table,
    wq_in, wk_in, wv_in, wo_in, wi_in, wf_in,
    pay, factors, n1_out, probs_out, dl_out, turned_out, yk_out, yv_out, qf_out, gctx_out, z_out, vz_out,
    ga_out, a2_out, fhat_out, yq_out,
    wq_out, wk_out, wv_out, wo_out, wi_out, wf_out,
    square, wide, wq, wk, wv, wo, wi, wf, padded, first, gather_z, logits, expand, wide_z,
    in_sems, out_sems,
):
    rows, length, width, pairs, heads, docs = dims
    count = rows * pairs
    n_in = [wq_in, wk_in, wv_in, wo_in]
    n_low = [wq, wk, wv, wo]
    n_out = [wq_out, wk_out, wv_out, wo_out]
    hidden = wi.shape[1]
    parts = hidden // width
    loads = [pltpu.make_async_copy(n_in[i], square.at[i], in_sems.at[i]) for i in range(4)]
    wide_load = pltpu.make_async_copy(wi_in, wide, in_sems.at[4])
    for load in loads:
        load.start()
    wide_load.start()

    gain = first_gain[...]
    for r in range(rows):
        padded[r, length:, :] = jnp.zeros((reach, width), bf16)

        def norm_step(i, carry, r=r):
            at = pl.ds(pl.multiple_of(i * 64, 64), 64)
            x = tokens[r, at, :]
            n = (x * rms_factor(x) * gain).astype(bf16)
            n1_out[r, at, :] = n
            padded[r, at, :] = n
            return carry

        lax.fori_loop(0, length // 64, norm_step, 0)
    first[...] = jnp.zeros(first.shape, f32)
    pieces = []
    for r in range(rows):
        for at, size in starts_of(lengths, r, pairs):
            p = len(pieces)
            shift = at & (group - 1)
            pieces.append((r, pl.multiple_of(at - shift, group), shift, size))
            first[p : p + 1, :] = tokens[r, pl.ds(at, 1), :]

    def nearby(p):
        r, base, _, _ = pieces[p]
        return padded[r, pl.ds(base, reach), :]

    spots = [slice(p * group, (p + 1) * group) for p in range(count)]
    head_rows = iota((group, width), 0) == lax.shift_right_logical(
        iota((group, width), 1), int(math.log2(width // heads))
    )

    def widen(values):
        for p in range(count):
            expand[p * group : (p + 1) * group, :] = jnp.where(
                head_rows, values[p : p + 1, :], 0.0
            ).astype(bf16)

    def narrow(target):
        target[...] = jnp.zeros(target.shape, f32)
        for p in range(count):
            block = wide_z[p * group : (p + 1) * group, :]
            target[p : p + 1, :] = jnp.sum(
                jnp.where(head_rows, block, 0.0), axis=0, keepdims=True
            )

    stores = []

    def take(i):
        loads[i].wait()
        cast_rows(n_low[i], square.at[i], 64)
        store = pltpu.make_async_copy(n_low[i], n_out[i], out_sems.at[i])
        store.start()
        stores.append(store)
        if i < parts:
            part = pltpu.make_async_copy(
                wf_in.at[pl.ds(i * width, width), :], square.at[i], in_sems.at[5 + i]
            )
            part.start()
            return part

    wf_loads = [take(0)]
    n1_first = (first[...] * rms_factor(first[...]) * gain).astype(bf16)
    q_first = mm(n1_first, wq[...]).astype(bf16)
    qf_out[...] = q_first
    widen(q_first.astype(f32))
    wf_loads.append(take(1))
    yk_out[...] = mm_nt(expand[...], wk[...]).astype(bf16)
    position = bias_vector(table[...], lanes_path, 0)
    position = jnp.concatenate([position, jnp.zeros((group - heads, lanes_path), f32)], axis=0)
    lane = iota((group, lanes_path), 1)
    for p, (_, _, shift, size) in enumerate(pieces):
        logits[spots[p], :reach] = mm_nt(yk_out[spots[p], :], nearby(p))
        block = logits[spots[p], :] + pltpu.roll(position, shift, 1)
        inside = jnp.logical_and(lane >= shift, lane < shift + size)
        logits[spots[p], :] = jnp.where(inside, block, negative)
    wf_loads.append(take(2))
    wf_loads.append(take(3))
    scores_in = logits[...]
    peak = jnp.max(scores_in, axis=-1, keepdims=True)
    raised = jnp.exp(scores_in - peak)
    probs = raised / jnp.sum(raised, axis=-1, keepdims=True)
    probs_out[...] = probs.astype(bf16)
    for p in range(count):
        vz_out[spots[p], :] = mm(probs_out[spots[p], :reach], nearby(p)).astype(bf16)
    wide_z[...] = mm(vz_out[...], wv[...])
    narrow(gather_z)
    context = gather_z[...].astype(bf16)
    attended = first[...] + mm(context, wo[...])
    scale_two = rms_factor(attended)
    second = attended * scale_two
    normed_two = (second * second_gain[...]).astype(bf16)
    wide_load.wait()
    cast_rows(wi, wide, 32)
    store = pltpu.make_async_copy(wi, wi_out, out_sems.at[4])
    store.start()
    stores.append(store)
    value, slope = gelu_pair(mm(normed_two, wi[...]))
    for i, load in enumerate(wf_loads):
        load.wait()
        cast_rows(wf.at[pl.ds(i * width, width), :], square.at[i], 64)
    store = pltpu.make_async_copy(wf, wf_out, out_sems.at[5])
    store.start()
    stores.append(store)
    encoded = attended + mm(value.astype(bf16), wf[...])
    scale_final = rms_factor(encoded)
    final_hat = encoded * scale_final
    fhat_out[...] = final_hat
    unit = score_vector[...] * final_gain[...]
    score_col = jnp.sum(final_hat * unit, axis=-1, keepdims=True)
    square_lane = iota((group, 128), 1)
    row = jnp.sum(
        jnp.where(square_lane == iota((group, 128), 0), score_col, 0.0), axis=0, keepdims=True
    )
    row_lane = iota((1, 128), 1)
    place = lax.axis_index("docs") * count
    for i in range(count):
        row = jnp.where(row_lane == group + i, ids[0, place + i].astype(f32), row)
        row = jnp.where(row_lane == 2 * group + i, labels[0, place + i].astype(f32), row)
    pay[...] = row

    grad_encoded = norm_back(final_hat, scale_final, jnp.broadcast_to(unit, final_hat.shape))
    grad_branch = grad_encoded.astype(bf16)
    grad_preact = (mm_nt(grad_branch, wf[...]) * slope).astype(bf16)
    grad_normed_two = mm_nt(grad_preact, wi[...])
    a2_out[...] = second * grad_normed_two
    grad_attended = grad_encoded + norm_back(second, scale_two, grad_normed_two * second_gain[...])
    ga_out[...] = grad_attended
    grad_attn = grad_attended.astype(bf16)
    grad_context = mm_nt(grad_attn, wo[...])
    gctx_out[...] = grad_context
    widen(grad_context)
    yv_out[...] = mm_nt(expand[...], wv[...]).astype(bf16)
    logits[...] = jnp.zeros(logits.shape, f32)
    for p in range(count):
        logits[spots[p], :reach] = mm_nt(yv_out[spots[p], :], nearby(p))
    grad_probs = logits[...]
    grad_logits = probs * (grad_probs - jnp.sum(probs * grad_probs, axis=-1, keepdims=True))
    dl_out[...] = grad_logits.astype(bf16)
    for p, (_, _, shift, _) in enumerate(pieces):
        rounded = dl_out[spots[p], :]
        z_out[spots[p], :] = mm(rounded[:, :reach], nearby(p))
        turned = pltpu.roll(rounded.astype(f32), (lanes_path - shift) & (lanes_path - 1), 1)
        turned_out[spots[p], :] = turned[:, :window]
    wide_z[...] = mm(z_out[...].astype(bf16), wk[...])
    narrow(gather_z)
    grad_query = gather_z[...].astype(bf16)
    yq_out[...] = mm_nt(grad_query, wq[...])
    for i, member in enumerate((n1_first, grad_query, context, grad_attn, normed_two, grad_branch)):
        factors[:, i * width : (i + 1) * width] = member
    for store in stores:
        store.wait()


def path_call(tokens, lengths, ids, labels, gains, table, weights):
    rows, length, width = tokens.shape
    pairs = lengths.shape[1]
    heads = table.shape[1]
    hidden = weights[4].shape[1]
    combos = rows * pairs * group
    shape = jax.ShapeDtypeStruct
    outs = [
        shape((1, 128), f32),
        shape((group, 6 * width), bf16),
        shape((rows, length, width), bf16),
        shape((combos, lanes_path), bf16),
        shape((combos, lanes_path), bf16),
        shape((combos, window), f32),
        shape((combos, width), bf16),
        shape((combos, width), bf16),
        shape((group, width), bf16),
        shape((group, width), f32),
        shape((combos, width), f32),
        shape((combos, width), bf16),
        shape((group, width), f32),
        shape((group, width), f32),
        shape((group, width), f32),
        shape((group, width), f32),
    ]
    low = [shape(w.shape, bf16) for w in weights]
    square_low = pltpu.VMEM((width, width), bf16)
    return pl.pallas_call(
        functools.partial(path_kernel, (rows, length, width, pairs, heads, None)),
        out_shape=outs + low,
        in_specs=[scalars] * 3 + [whole] * 6 + [anywhere] * 6,
        out_specs=[whole] * len(outs) + [anywhere] * 6,
        scratch_shapes=[
            pltpu.VMEM((4, width, width), f32),
            pltpu.VMEM((width, hidden), f32),
            square_low, square_low, square_low, square_low,
            pltpu.VMEM((width, hidden), bf16),
            pltpu.VMEM((hidden, width), bf16),
            pltpu.VMEM((rows, length + reach, width), bf16),
            pltpu.VMEM((group, width), f32),
            pltpu.VMEM((group, width), f32),
            pltpu.VMEM((combos, lanes_path), f32),
            pltpu.VMEM((combos, width), bf16),
            pltpu.VMEM((combos, width), f32),
            pltpu.SemaphoreType.DMA((9,)),
            pltpu.SemaphoreType.DMA((6,)),
        ],
        compiler_params=pltpu.CompilerParams(vmem_limit_bytes=58 << 20),
        cost_estimate=pl.CostEstimate(flops=int(9e9), bytes_accessed=int(5e7), transcendentals=0),
        name="path",
    )(lengths, ids, labels, tokens, *gains, table, *weights)


def code_of(stages, indices):
    total = len(stages)
    code = 0
    for s, (axis, mask) in enumerate(stages):
        bit = jnp.where((indices[axis] & mask) != 0, 1, 0) if not isinstance(
            indices[axis], int
        ) else (1 if indices[axis] & mask else 0)
        code = code + bit * (1 << (total - 1 - s))
    return code


def cut_stages(stages, width):
    count = 0
    while count < len(stages) and (2 * width) % (group << (count + 1)) == 0:
        count += 1
    return stages[:count]


def own_code(stages):
    return code_of(stages, {axis: lax.axis_index(axis) for axis in ("docs", "lists")})


def terms_kernel(
    dims,
    pay, z, vz, qf, gctx, dl, a2, fhat, final_gain, score_vector,
    keep, send, g_all, g_own, smalls,
    ranked, term, left, right,
):
    stages, docs, lists, list_count, count, heads, buckets = dims
    devices = docs * lists
    width = z.shape[1]
    me = own_code(stages)
    everything = pay[...]
    lane = iota(everything.shape, 1)
    score = everything
    names = pltpu.roll(everything, 128 - group, 1)
    label = pltpu.roll(everything, 128 - 2 * group, 1)
    used = lane < count
    part = lax.shift_right_logical(iota(everything.shape, 0), int(math.log2(docs)))
    key = jnp.where(used, part * list_count + names.astype(jnp.int32), -1)

    def total_of(values):
        return jnp.sum(jnp.sum(values, axis=1, keepdims=True), axis=0, keepdims=True)

    def top_step(k, top):
        member = key == k
        best = jnp.max(
            jnp.max(jnp.where(member, score, negative), axis=1, keepdims=True),
            axis=0, keepdims=True,
        )
        return jnp.where(member, best, top)

    keys = lists * list_count
    unroll = keys if keys <= 16 else 4
    top = lax.fori_loop(0, keys, top_step, score, unroll=unroll)
    raised = jnp.exp(score - top)

    def sum_step(k, carry):
        total, gain = carry
        member = key == k
        return (
            jnp.where(member, total_of(jnp.where(member, raised, 0.0)), total),
            jnp.where(member, total_of(jnp.where(member, label, 0.0)), gain),
        )

    ones = jnp.ones(everything.shape, f32)
    total, gain = lax.fori_loop(0, keys, sum_step, (ones, ones), unroll=unroll)
    grads = jnp.where(used, raised / total * gain - label, 0.0)
    ranked[...] = grads
    for d in range(devices):
        code = code_of(stages, {"docs": d // lists, "lists": d % lists})
        g_all[d : d + 1, :] = ranked[pl.ds(me ^ code, 1), :]
    own = ranked[0:1, :]
    g_own[...] = jnp.broadcast_to(own, g_own.shape)

    combos = count * group
    pair_of = lax.shift_right_logical(iota((combos, 128), 0), int(math.log2(group)))
    g_combo = jnp.sum(jnp.where(iota((combos, 128), 1) == pair_of, own, 0.0), axis=1, keepdims=True)
    g_pair = jnp.sum(
        jnp.where(iota((group, 128), 1) == iota((group, 128), 0), own, 0.0), axis=1, keepdims=True
    )
    head_rows = iota((group, width), 0) == lax.shift_right_logical(
        iota((group, width), 1), int(math.log2(width // heads))
    )
    queries = qf[...].astype(f32)
    upstream = gctx[...] * g_pair
    for p in range(count):
        at = slice(p * group, (p + 1) * group)
        right[0, at, :] = jnp.where(head_rows, queries[p : p + 1, :], 0.0).astype(bf16)
        right[1, at, :] = jnp.where(head_rows, upstream[p : p + 1, :], 0.0).astype(bf16)
    left[...] = (z[...] * g_combo).astype(bf16)
    term[0:width, :] = mm_tn(left[...], right[0])
    term[width : 2 * width, :] = mm_tn(vz[...], right[1])

    half, piece = keep.shape[0], keep.shape[1]
    blocks = width // piece
    mine = own_code(stages[: half.bit_length()])

    def piece_step(r, carry, target, base):
        owner = mine ^ (base + r)
        side = lax.shift_right_logical(owner, int(math.log2(blocks)))
        at = side * width + (owner & (blocks - 1)) * piece
        target[r] = term[pl.ds(pl.multiple_of(at, group), piece), :].astype(bf16)
        return carry

    lax.fori_loop(0, half, functools.partial(piece_step, target=send, base=half), 0)
    lax.fori_loop(0, half, functools.partial(piece_step, target=keep, base=0), 0)

    smalls[...] = jnp.zeros(smalls.shape, f32)
    smalls[0:1, :] = jnp.sum(a2[...] * g_pair, axis=0, keepdims=True)
    hats = jnp.sum(fhat[...] * g_pair, axis=0, keepdims=True)
    smalls[1:2, :] = hats * score_vector[...]
    smalls[2:3, :] = hats * final_gain[...]
    weighted = dl[...] * g_combo
    summed = weighted[0:group, :]
    for p in range(1, count):
        summed = summed + weighted[p * group : (p + 1) * group, :]
    spots = iota((window, width), 1)
    hot = jnp.where(bucket_of(iota((window, width), 0)) == (spots & (buckets - 1)), 1.0, 0.0)
    spread = lax.dot_general(
        summed, hot, (((1,), (0,)), ((), ())), precision=highest, preferred_element_type=f32
    )
    row_of = lax.shift_right_logical(iota((group, width), 1), int(math.log2(buckets)))
    smalls[3:4, :] = jnp.sum(
        jnp.where(row_of == iota((group, width), 0), spread, 0.0), axis=0, keepdims=True
    )


def terms_call(dims, pay, z, vz, qf, gctx, dl, a2, fhat, final_gain, score_vector):
    stages, docs, lists, list_count, count, heads, buckets = dims
    devices = docs * lists
    combos, width = z.shape
    pieces = 1 << len(cut_stages(stages, width))
    piece = 2 * width // pieces
    shape = jax.ShapeDtypeStruct
    half = shape((pieces // 2, piece, width), bf16)
    return pl.pallas_call(
        functools.partial(terms_kernel, dims),
        out_shape=[
            half, half,
            shape((devices, 128), f32),
            shape((8, 128), f32),
            shape((8, width), f32),
        ],
        in_specs=[whole] * 10,
        out_specs=[whole] * 5,
        scratch_shapes=[
            pltpu.VMEM((devices, 128), f32),
            pltpu.VMEM((2 * width, width), f32),
            pltpu.VMEM((combos, width), bf16),
            pltpu.VMEM((2, combos, width), bf16),
        ],
        compiler_params=pltpu.CompilerParams(vmem_limit_bytes=24 << 20),
        cost_estimate=pl.CostEstimate(flops=int(4e9), bytes_accessed=int(1e7), transcendentals=0),
        name="terms",
    )(pay, z, vz, qf, gctx, dl, a2, fhat, final_gain, score_vector)


def attention_kernel(
    dims,
    lengths, n1, tokens, table, wq_in, wk_in, wv_in, wo_in,
    out,
    wq, wk, wv, wo, q, k, v, ctx, bias, sems,
):
    row, heads, pairs = dims
    length, width = n1.shape[1], n1.shape[2]
    names = ((wq_in, wq), (wk_in, wk), (wv_in, wv), (wo_in, wo))
    loads = [pltpu.make_async_copy(a, b, sems.at[i]) for i, (a, b) in enumerate(names)]
    for load in loads:
        load.start()
    lanes = 4 * window
    vector = bias_vector(table[...], lanes, window)
    for h in range(heads):
        bias[h] = pltpu.roll(
            jnp.broadcast_to(vector[h : h + 1, :], (window, lanes)), 0, 1, stride=1, stride_axis=0
        )[:, : 3 * window]
    x = n1[0]
    for load, target, low in ((loads[0], q, wq), (loads[1], k, wk), (loads[2], v, wv)):
        load.wait()
        target[...] = mm(x, low[...]).astype(bf16)
    tiles = length // window
    half = iota((2 * window, window), 1) < (width // heads)
    left = half[:window]
    upper = iota((2 * window, window), 0) < window
    chosen = half == upper
    ends = []
    at = 0
    for i in range(pairs):
        at = at + lengths[row, i]
        ends.append(at)

    def segment(positions):
        total = jnp.zeros(positions.shape, jnp.int32)
        for end in ends:
            total = total + jnp.where(positions >= end, 1, 0)
        return total

    for j in range(tiles):
        t0 = j * window
        k0 = max(j - 1, 0) * window
        k1 = min(j + 2, tiles) * window
        off = k0 - (t0 - window)
        span = k1 - k0
        seg_q = segment(t0 + iota((window, 1), 0))
        seg_k = segment(k0 + iota((1, span), 1))
        allowed = seg_q == seg_k
        for pair in range(heads // 2):
            cols = slice(pair * window, (pair + 1) * window)
            both = q[t0 : t0 + window, cols]
            stacked = jnp.concatenate([both, both], axis=0)
            stacked = jnp.where(chosen, stacked, jnp.zeros_like(stacked))
            raw = mm_nt(stacked, k[k0:k1, cols])
            probs, sums = [], []
            for side in range(2):
                part = raw[side * window : (side + 1) * window]
                part = part + bias[2 * pair + side, :, off : off + span]
                part = jnp.where(allowed, part, negative)
                peak = jnp.max(part, axis=-1, keepdims=True)
                raised = jnp.exp(part - peak)
                sums.append(jnp.sum(raised, axis=-1, keepdims=True))
                probs.append(raised.astype(bf16))
            mixed = mm(jnp.concatenate(probs, axis=0), v[k0:k1, cols])
            ctx[t0 : t0 + window, cols] = jnp.where(
                left, mixed[:window] / sums[0], mixed[window:] / sums[1]
            ).astype(bf16)
    loads[3].wait()
    out[0] = tokens[0] + mm(ctx[...], wo[...])


def attention_call(row, lengths, n1, tokens, table, weights):
    rows, length, width = tokens.shape
    heads = table.shape[1]
    pairs = lengths.shape[1]
    square = pltpu.VMEM((width, width), bf16)
    tall = pltpu.VMEM((length, width), bf16)
    block = pl.BlockSpec((1, length, width), lambda i: (row, 0, 0))
    return pl.pallas_call(
        functools.partial(attention_kernel, (row, heads, pairs)),
        grid=(1,),
        out_shape=jax.ShapeDtypeStruct((1, length, width), f32),
        in_specs=[scalars, block, block, whole] + [anywhere] * 4,
        out_specs=pl.BlockSpec((1, length, width), lambda i: (0, 0, 0)),
        scratch_shapes=[square] * 4 + [tall] * 4 + [
            pltpu.VMEM((heads, window, 3 * window), f32),
            pltpu.SemaphoreType.DMA((4,)),
        ],
        compiler_params=pltpu.CompilerParams(vmem_limit_bytes=32 << 20),
        cost_estimate=pl.CostEstimate(flops=int(9e9), bytes_accessed=int(1e7), transcendentals=0),
        name=f"attention_{row}",
    )(lengths, n1, tokens, table, *weights)


def feed_kernel(attended, gain, wi, wf, held, out, normed, total):
    step = pl.program_id(0)

    @pl.when(step == 0)
    def _():
        x = attended[0]
        normed[...] = (x * rms_factor(x) * gain[...]).astype(bf16)
        total[...] = x

    value = gelu(mm(normed[...], wi[...])).astype(bf16)
    total[...] += mm(value, wf[...])

    @pl.when(step == pl.num_programs(0) - 1)
    def _():
        out[0] = total[...]


def feed_call(row, shape, attended, gain, wi, wf, held):
    rows, length, width = shape
    hidden = wi.shape[1]
    chunk = 768
    still = lambda i: (0, 0, 0)
    extra = [] if held is None else [held]
    kernel = feed_kernel
    if held is None:
        kernel = lambda a, g, i, f, o, n, t: feed_kernel(a, g, i, f, None, o, n, t)
    return pl.pallas_call(
        kernel,
        grid=(hidden // chunk,),
        out_shape=jax.ShapeDtypeStruct(shape, f32),
        in_specs=[
            pl.BlockSpec((1, length, width), still),
            pl.BlockSpec((1, width), lambda i: (0, 0)),
            pl.BlockSpec((width, chunk), lambda i: (0, i)),
            pl.BlockSpec((chunk, width), lambda i: (i, 0)),
        ] + [anywhere] * len(extra),
        out_specs=pl.BlockSpec((1, length, width), lambda i: (row, 0, 0)),
        input_output_aliases={4: 0} if extra else {},
        scratch_shapes=[pltpu.VMEM((length, width), bf16), pltpu.VMEM((length, width), f32)],
        compiler_params=pltpu.CompilerParams(vmem_limit_bytes=32 << 20),
        cost_estimate=pl.CostEstimate(flops=int(6e9), bytes_accessed=int(1e7), transcendentals=0),
        name=f"feed_{row}",
    )(attended, gain, wi, wf, *extra)


def tokens_grad_kernel(
    dims, lengths, tokens, g_own, probs, dl, yk, yv, yq, ga, gain, out, first_sum, spread
):
    length, width, pairs = dims
    row = pl.program_id(0)
    spread[...] = jnp.zeros(spread.shape, f32)
    own = g_own[0:1, :]
    lane = iota((1, 128), 1)
    starts = starts_of(lengths, row, pairs)
    amounts = []
    for i, (at, size) in enumerate(starts):
        pair = row * pairs + i
        amount = jnp.sum(jnp.where(lane == pair, own, 0.0), axis=1, keepdims=True)
        amounts.append(amount)
        here = pl.ds(pl.multiple_of(pair * group, group), group)
        left = jnp.concatenate([dl[here, :], probs[here, :]], axis=0)
        right = jnp.concatenate([yk[here, :], yv[here, :]], axis=0)
        base = pl.multiple_of(at - (at & (group - 1)), group)
        spread[pl.ds(base, reach), :] += mm_tn(left, right)[:reach] * amount
    for i, (at, size) in enumerate(starts):
        pair = row * pairs + i
        spread[pl.ds(at, 1), :] += yq[pl.ds(pair, 1), :] * amounts[i]

    @pl.when(row == 0)
    def _():
        first_sum[...] = jnp.zeros(first_sum.shape, f32)

    def step(i, carry):
        at = pl.ds(pl.multiple_of(i * 64, 64), 64)
        x = tokens[0, at, :]
        factor = rms_factor(x)
        hat = x * factor
        upstream = spread[at, :]
        out[0, at, :] = norm_back(hat, factor, upstream * gain[...])
        return carry + jnp.sum(hat * upstream, axis=0, keepdims=True)

    first_sum[...] += lax.fori_loop(0, length // 64, step, jnp.zeros((1, width), f32))
    for i, (at, size) in enumerate(starts):
        pair = row * pairs + i
        out[0, pl.ds(at, 1), :] += ga[pl.ds(pair, 1), :] * amounts[i]


def tokens_grad_call(lengths, tokens, g_own, probs, dl, yk, yv, yq, ga, gain):
    rows, length, width = tokens.shape
    pairs = lengths.shape[1]
    block = pl.BlockSpec((1, length, width), lambda i: (i, 0, 0))
    return pl.pallas_call(
        functools.partial(tokens_grad_kernel, (length, width, pairs)),
        grid=(rows,),
        out_shape=[
            jax.ShapeDtypeStruct(tokens.shape, f32),
            jax.ShapeDtypeStruct((1, width), f32),
        ],
        in_specs=[scalars, block] + [whole] * 8,
        out_specs=[block, pl.BlockSpec((1, width), lambda i: (0, 0))],
        scratch_shapes=[pltpu.VMEM((length + reach, width), f32)],
        compiler_params=pltpu.CompilerParams(vmem_limit_bytes=32 << 20),
        cost_estimate=pl.CostEstimate(flops=int(2e9), bytes_accessed=int(1e7), transcendentals=0),
        name="tokens_grad",
    )(lengths, tokens, g_own, probs, dl, yk, yv, yq, ga, gain)


def outer_kernel(
    blocks, factors, g, wi, wf, inner_out, outer_out, output_out, query_out, branch, normed
):
    step, block = pl.program_id(0), pl.program_id(1)
    width = branch.shape[1]

    def member(i):
        return factors[:, i * width : (i + 1) * width]

    def put(target, values):
        if blocks == 1:
            target[...] = values
        else:
            target[...] = jnp.where(block == 0, values, target[...] + values)

    def prepare():
        branch[...] = (member(5).astype(f32) * g[...]).astype(bf16)
        normed[...] = member(4)

    @pl.when(step == 0)
    def _():
        if blocks == 1:
            prepare()
        put(query_out, mm_tn(member(0), (member(1).astype(f32) * g[...]).astype(bf16)))
        put(output_out, mm_tn(member(2), (member(3).astype(f32) * g[...]).astype(bf16)))

    if blocks > 1:
        prepare()
    value, slope = gelu_pair(mm(normed[...], wi[...]))
    grad = (mm_nt(branch[...], wf[...]) * slope).astype(bf16)
    put(inner_out, mm_tn(normed[...], grad))
    put(outer_out, mm_tn(value.astype(bf16), branch[...]))


def outer_call(factors, g, wi, wf):
    rows = factors.shape[0]
    width, hidden = wi.shape
    chunk = 384
    block = min(rows, 512)
    blocks = rows // block
    shape = jax.ShapeDtypeStruct
    fixed = lambda i, b: (0, 0)
    return pl.pallas_call(
        functools.partial(outer_kernel, blocks),
        grid=(hidden // chunk, blocks),
        out_shape=[
            shape((width, hidden), f32),
            shape((hidden, width), f32),
            shape((width, width), f32),
            shape((width, width), f32),
        ],
        in_specs=[
            pl.BlockSpec((block, 6 * width), lambda i, b: (b, 0)),
            pl.BlockSpec((block, 1), lambda i, b: (b, 0)),
            pl.BlockSpec((width, chunk), lambda i, b: (0, i)),
            pl.BlockSpec((chunk, width), lambda i, b: (i, 0)),
        ],
        out_specs=[
            pl.BlockSpec((width, chunk), lambda i, b: (0, i)),
            pl.BlockSpec((chunk, width), lambda i, b: (i, 0)),
            pl.BlockSpec((width, width), fixed),
            pl.BlockSpec((width, width), fixed),
        ],
        scratch_shapes=[pltpu.VMEM((block, width), bf16), pltpu.VMEM((block, width), bf16)],
        compiler_params=pltpu.CompilerParams(vmem_limit_bytes=48 << 20),
        cost_estimate=pl.CostEstimate(flops=int(11e9), bytes_accessed=int(4e7), transcendentals=0),
        name="outer",
    )(factors, g, wi, wf)


def last_kernel(dims, gathered, key_out, value_out, small_out):
    stages, devices, piece = dims
    width = key_out.shape[1]
    me = own_code(stages)
    blocks = width // piece
    sides = (key_out, value_out)

    def step(i, carry):
        at = pl.ds(pl.multiple_of(i * piece, group), piece)
        for side in range(2):
            slot = me ^ (side * blocks + i)
            sides[side][at, :] = gathered[slot, :piece, :].astype(f32)
        return carry

    lax.fori_loop(0, blocks, step, 0)

    def add(i, carry):
        return carry + gathered[i, piece:, :].astype(f32)

    small_out[...] = lax.fori_loop(0, devices, add, jnp.zeros(small_out.shape, f32))


def last_call(stages, gathered, piece):
    devices, rows, width = gathered.shape
    shape = jax.ShapeDtypeStruct
    return pl.pallas_call(
        functools.partial(last_kernel, (stages, devices, piece)),
        out_shape=[
            shape((width, width), f32),
            shape((width, width), f32),
            shape((rows - piece, width), f32),
        ],
        in_specs=[whole],
        out_specs=[whole] * 3,
        compiler_params=pltpu.CompilerParams(vmem_limit_bytes=32 << 20),
        cost_estimate=pl.CostEstimate(flops=int(1e7), bytes_accessed=int(1e7), transcendentals=0),
        name="last",
    )(gathered)


def shards(
    docs, lists,
    tokens, pair_lengths, list_ids, relevance,
    first_gain, query_weight, key_weight, value_weight, output_weight, bias_table,
    second_gain, inner_weight, outer_weight, final_gain, score_vector,
):
    row_count, length, width = tokens.shape[1:]
    pairs = pair_lengths.shape[2]
    buckets, heads = bias_table.shape
    devices = docs * lists
    sizes = {"docs": docs, "lists": lists}
    stages = tuple(("lists", 1 << b) for b in range(lists.bit_length() - 1)) + tuple(
        ("docs", 1 << b) for b in range(docs.bit_length() - 1)
    )

    def swap(values, stage):
        axis, mask = stage
        return lax.ppermute(values, axis, [(i, i ^ mask) for i in range(sizes[axis])])

    rows = tokens.reshape(row_count, length, width)
    lengths = pair_lengths.reshape(row_count, pairs)
    flat = lambda vector: vector.reshape(1, width)
    gains = (flat(first_gain), flat(second_gain), flat(final_gain), flat(score_vector))
    outs = path_call(
        rows, lengths, list_ids, relevance, gains, bias_table,
        (query_weight, key_weight, value_weight, output_weight, inner_weight, outer_weight),
    )
    pay, factors, n1, probs, dl, turned, yk, yv, qf, gctx, z, vz, ga, a2, fhat, yq = outs[:16]
    wq, wk, wv, wo, wi, wf = outs[16:]

    gathered_rows = lax.all_gather(factors, ("docs", "lists"), axis=0, tiled=True)

    for stage in reversed(stages):
        pay = jnp.concatenate([pay, swap(pay, stage)], axis=0)
    count = row_count * pairs
    dims = (stages, docs, lists, docs // 2, count, heads, buckets)
    keep, send, g_all, g_own, smalls = terms_call(
        dims, pay, z, vz, qf, gctx, turned, a2, fhat, gains[2], gains[3]
    )
    piece = keep.shape[1]
    g_rows = g_all[:, :group].reshape(devices * group, 1)

    cut = cut_stages(stages, width)
    for i, stage in enumerate(cut):
        if i:
            half = keep.shape[0] // 2
            keep, send = keep[:half], keep[half:]
        keep = keep + swap(send, stage)
    for stage in stages[len(cut) :]:
        keep = keep + swap(keep, stage)

    weights = (wq, wk, wv, wo)
    grads, first_sum = tokens_grad_call(
        lengths, rows, g_own, probs, dl, yk, yv, yq, ga, gains[0]
    )
    encoded = None
    for r in range(row_count):
        attended = attention_call(r, lengths, n1, rows, bias_table, weights)
        encoded = feed_call(r, rows.shape, attended, gains[1], wi, wf, encoded)
    inner_grad, outer_grad, output_grad, query_grad = outer_call(gathered_rows, g_rows, wi, wf)

    smalls = jnp.concatenate([smalls[:4], first_sum, smalls[5:]], axis=0)
    for stage in stages[len(cut) :]:
        smalls = smalls + swap(smalls, stage)
    gathered = jnp.concatenate([keep, smalls.astype(bf16)[None]], axis=1)
    for stage in reversed(cut):
        gathered = jnp.concatenate([gathered, swap(gathered, stage)], axis=0)
    key_grad, value_grad, small_sums = last_call(cut, gathered, piece)
    table_grad = small_sums[3, : heads * buckets].reshape(heads, buckets).T
    scores = outs[0][:, :count]
    return (
        encoded.reshape(tokens.shape),
        scores.reshape(1, row_count, pairs),
        grads.reshape(tokens.shape),
        small_sums[4],
        query_grad,
        key_grad,
        value_grad,
        output_grad,
        table_grad,
        small_sums[0],
        inner_grad,
        outer_grad,
        small_sums[1],
        small_sums[2],
    )


def solution(mesh):
    placed = P("lists", "docs", None, None)
    return jax.shard_map(
        functools.partial(shards, mesh.shape["docs"], mesh.shape["lists"]),
        mesh=mesh,
        in_specs=(placed, P("lists", "docs", None), P("lists", None), P("lists", None)) + (P(),) * 11,
        out_specs=(placed, P("lists", "docs", None), placed) + (P(),) * 11,
        check_vma=False,
    )
```

time: 1340 us -> 226 us (0.17)
  blocking collectives: 504 us -> 0 us
  waiting for transfers between devices: 325 us -> 58.5 us
  local copies, waits for them, and re-layouts: 228 us -> 31.5 us
  matrix products: 149 us -> 0 us
  Pallas kernels: 0 us -> 95 us
  other arithmetic: 93.9 us -> 4.09 us
  starting transfers between devices: 0.25 us -> 20.8 us
    psum x1 -> x0, blocking collectives: 461 us -> none  [shards(): lax.psum((grad_table, grad_first, grad_second, grad_final, grad_vector),...]
    all_gather x6 -> x1, waiting for transfers between devices: 325 us -> 0.01 us  [shards(): lax.all_gather(factors, ('docs', 'lists'), axis=0, tiled=True)]
    dot_general x45 -> x0, matrix products: 149 us -> none  [the longest x10 26.1 us: times_transpose(): lax.dot_general(left_rows, right_rows, (((1,), (1,)), ((), ())), preferre...]
    pallas_call x0 -> x9, Pallas kernels: none -> 95 us  [the longest x1 24.8 us: path_call(): pl.pallas_call(functools.partial(path_kernel, (rows, length, width, pairs...]
    ppermute x0 -> x15, waiting for transfers between devices: none -> 58.5 us  [swap(): lax.ppermute(values, axis, [(i, i ^ mask) for i in range(sizes[axis])])]
    gather x24 -> x0, local copies, waits for them, and re-layouts: 56.8 us -> none  [the longest x2 14 us: backward_row(): position_bias[:, starts, :]]
    reshape x19 -> x6, local copies, waits for them, and re-layouts: 53.5 us -> 5.87 us  [the longest x4 5.07 us: shards(): flat = lambda vector: vector.reshape(1, width)]
    unnamed x1 -> x0, blocking collectives: 43.5 us -> none
  transfers between devices with their start and end apart: 6 -> 16, of which waited for: 6 -> 13; matrix products, arithmetic and copies ran while one was open for 2% -> 6% of each run, Pallas kernels for 0% -> 23%
where the time goes in v1:
time: 226 us; the launch traced here: 224 us
  Pallas kernels  95 us (42%)
  waiting for transfers between devices  58.5 us (26%)
  local copies, waits for them, and re-layouts  31.5 us (14%)
  starting transfers between devices  20.8 us (9%)
  between operations  14.5 us (6%)
  other arithmetic  4.09 us (2%)
    ppermute x15, waiting for transfers between devices, swap(): lax.ppermute(values, axis, [(i, i ^ mask) for i in range(sizes[axis])])  58.5 us
    pallas_call x1, Pallas kernels, path_call(): pl.pallas_call(functools.partial(path_kernel, (rows, length, width, pairs...  24.8 us
    pallas_call x2, Pallas kernels, attention_call(): pl.pallas_call(functools.partial(attention_kernel, (row, heads, pairs)),...  23.2 us
    ppermute x15, starting transfers between devices, swap(): lax.ppermute(values, axis, [(i, i ^ mask) for i in range(sizes[axis])])  20.8 us
    unnamed x87, local copies, waits for them, and re-layouts  19.4 us
    pallas_call x1, Pallas kernels, outer_call(): pl.pallas_call(functools.partial(outer_kernel, blocks), grid=(hidden // c...  19.1 us
    pallas_call x2, Pallas kernels, feed_call(): pl.pallas_call(kernel, grid=(hidden // chunk,), out_shape=jax.ShapeDtypeS...  16.3 us
    pallas_call x1, Pallas kernels, tokens_grad_call(): pl.pallas_call(functools.partial(tokens_grad_kernel, (length, width, pair...  6.8 us
  transfers between devices with their start and end apart: 16, of which 13 were waited for; matrix products, arithmetic and copies ran while one was open for 6% of the time, Pallas kernels for 23%

profile of v1, /device:TPU:0, one launch (start us, length us, event | category | flops | bytes accessed | tf_op | source)
XLA Modules:
  0.0 224.5 jit_solution(3762135699272953409)
XLA Ops:
  13.7 24.8 %path.1 = (f32[1,128]{1,0:T(1,128)}, bf16[16,4608]{1,0:T(8,128)(2,1)}, bf16[2,512,768]{2,1,0:T(8,128)(2,1)}, bf16[192,256]{1,0:T(8,128)(2,1)}, bf16[192,256]{1,0...) custom-call(s32[2,6]{1,0:T(2,128)} %bitcast.17, ...), custom_call_target="tpu_custom_call" | custom-call | flops 8999999488 | bytes 50000000 | tf_op jit(solution)/shard_map/path/pallas_call | solution.py:306
  38.5 4.1 %collective-permute-start = (f32[1,128]{1,0:T(1,128)}, f32[1,128]{1,0:T(1,128)S(1)}, u32[]{:S(2)}, u32[]{:S(2)}) collective-permute-start(f32[1,128]{1,0:T(1,128)} %get-tuple-element.57), channel_id=1, source_target_pairs={{0,16},{2,18},{4,20},{6,22},{8,24},{10,26},{12,28},{14,30},{16,0},... | collective-permute-start | bytes 1544 | tf_op jit(solution)/shard_map/ppermute | solution.py:818
  44.9 1.9 collective-permute-start.1
  65.7 2.1 terms.1
  68.0 2.7 %collective-permute-done.5 = bf16[16,48,768]{2,1,0:T(8,128)(2,1)S(1)} collective-permute-done((bf16[16,48,768]{2,1,0:T(8,128)(2,1)S(1)}, bf16[16,48,768]{2,1,0:T(8,128)(2,1)S(1)}, u32[]{:S(2)}, u32[]{:S(2)}) %collective-permute-start.5) | collective-permute-done | bytes 1179680 | tf_op jit(solution)/shard_map/ppermute | solution.py:818
  71.1 1.9 collective-permute-start.6
  73.0 13.8 %collective-permute-done.6 = bf16[8,48,768]{2,1,0:T(8,128)(2,1)S(1)} collective-permute-done((bf16[8,48,768]{2,1,0:T(8,128)(2,1)S(1)}, bf16[8,48,768]{2,1,0:T(8,128)(2,1)S(1)}, u32[]{:S(2)}, u32[]{:S(2)}) %collective-permute-start.6) | collective-permute-done | bytes 589856 | tf_op jit(solution)/shard_map/ppermute | solution.py:818
  88.6 13.7 %collective-permute-done.7 = bf16[4,48,768]{2,1,0:T(8,128)(2,1)S(1)} collective-permute-done((bf16[4,48,768]{2,1,0:T(8,128)(2,1)S(1)}, bf16[4,48,768]{2,1,0:T(8,128)(2,1)S(1)}, u32[]{:S(2)}, u32[]{:S(2)}) %collective-permute-start.7) | collective-permute-done | bytes 294944 | tf_op jit(solution)/shard_map/ppermute | solution.py:818
  104.0 6.8 %tokens_grad.1 = (f32[2,512,768]{2,1,0:T(8,128)}, f32[1,768]{1,0:T(1,128)S(1)}) custom-call(s32[2,6]{1,0:T(2,128)S(1)} %bitcast.18, f32[2,512,768]{2,1,0:T(8,128)S(1)} %bitcast.14, f32[8,128]{1,0:T(8,128)S(1)} %get-tuple-element.65.g_own, bf16[192,256]{1,0:T(8,128)(2,1)S(1)} %copy-done.23, bf16[192,256]{1,0:T(8,128)(2,1)S(1)} %copy-done.24, ...), custom_call_target="tpu_custom_call" | custom-call | flops 2000000000 | bytes 10000000 | tf_op jit(solution)/shard_map/tokens_grad/pallas_call | solution.py:675
  111.0 2.4 %collective-permute-start.9 = (bf16[1,48,768]{2,1,0:T(8,128)(2,1)S(1)}, bf16[1,48,768]{2,1,0:T(8,128)(2,1)S(1)}, u32[]{:S(2)}, u32[]{:S(2)}) collective-permute-start(bf16[1,48,768]{2,1,0:T(8,128)(2,1)S(1)} %slice.77), channel_id=1, source_target_pairs={{0,16},{2,18},{4,20},{6,22},{8,24},{10,26},{12,28},{14,30},{16,0},... | collective-permute-start | bytes 221192 | tf_op jit(solution)/shard_map/ppermute | solution.py:818
  113.4 4.1 %collective-permute-done.9 = bf16[1,48,768]{2,1,0:T(8,128)(2,1)S(1)} collective-permute-done((bf16[1,48,768]{2,1,0:T(8,128)(2,1)S(1)}, bf16[1,48,768]{2,1,0:T(8,128)(2,1)S(1)}, u32[]{:S(2)}, u32[]{:S(2)}) %collective-permute-start.9) | collective-permute-done | bytes 73760 | tf_op jit(solution)/shard_map/ppermute | solution.py:818
  119.4 5.1 %collective-permute-done.10 = bf16[1,56,768]{2,1,0:T(8,128)(2,1)S(1)} collective-permute-done((bf16[1,56,768]{2,1,0:T(8,128)(2,1)S(1)}, bf16[1,56,768]{2,1,0:T(8,128)(2,1)S(1)}, u32[]{:S(2)}, u32[]{:S(2)}) %collective-permute-start.10) | collective-permute-done | bytes 86048 | tf_op jit(solution)/shard_map/ppermute | solution.py:818
  124.6 5.4 %collective-permute-done.11 = bf16[2,56,768]{2,1,0:T(8,128)(2,1)S(1)} collective-permute-done((bf16[2,56,768]{2,1,0:T(8,128)(2,1)S(1)}, bf16[2,56,768]{2,1,0:T(8,128)(2,1)S(1)}, u32[]{:S(2)}, u32[]{:S(2)}) %collective-permute-start.11) | collective-permute-done | bytes 172064 | tf_op jit(solution)/shard_map/ppermute | solution.py:818
  130.0 2.0 collective-permute-start.12
  132.2 11.6 %attention_0.1.a = f32[1,512,768]{2,1,0:T(8,128)S(1)} custom-call(s32[2,6]{1,0:T(2,128)S(1)} %bitcast.19, bf16[2,512,768]{2,1,0:T(8,128)(2,1)S(1)} %copy-done.9, f32[2,512,768]{2,1,0:T(8,128)S(1)} %bitcast.15, f32[32,12]{1,0:T(8,128)S(1)} %copy-done, bf16[768,768]{1,0:T(8,128)(2,1)S(1)} %copy-done.11, bf16[768,768]{1,0:T(8,128)(2,1)S(1)} %copy-done.13, ...), custom_call_target="tpu_custom_call" | custom-call | flops 8999999488 | bytes 10000000 | tf_op jit(solution)/shard_map/attention_0/pallas_call | solution.py:568
  144.7 8.2 %feed_0.1.held = f32[2,512,768]{2,1,0:T(8,128)} custom-call(f32[1,512,768]{2,1,0:T(8,128)S(1)} %attention_0.1.a, f32[1,768]{1,0:T(1,128)S(1)} %copy-done.1, bf16[768,3072]{1,0:T(8,128)(2,1)S(1)} %bitcast.22, bf16[3072,768]{1,0:T(8,128)(2,1)S(1)} %bitcast.26), custom_call_target="tpu_custom_call" | custom-call | flops 6000000000 | bytes 10000000 | tf_op jit(solution)/shard_map/feed_0/pallas_call | solution.py:610
  155.7 5.5 %collective-permute-done.13 = bf16[8,56,768]{2,1,0:T(8,128)(2,1)} collective-permute-done((bf16[8,56,768]{2,1,0:T(8,128)(2,1)}, bf16[8,56,768]{2,1,0:T(8,128)(2,1)}, u32[]{:S(2)}, u32[]{:S(2)}) %collective-permute-start.13) | collective-permute-done | bytes 688160 | tf_op jit(solution)/shard_map/ppermute | solution.py:818
  161.2 2.0 constant_dynamic-update-slice_fusion
  164.9 2.0 copy-done.12
  170.7 11.6 %attention_1.1.attended = f32[1,512,768]{2,1,0:T(8,128)S(1)} custom-call(s32[2,6]{1,0:T(2,128)S(1)} %bitcast.20, bf16[2,512,768]{2,1,0:T(8,128)(2,1)S(1)} %copy-done.10, f32[2,512,768]{2,1,0:T(8,128)S(1)} %bitcast.16, f32[32,12]{1,0:T(8,128)S(1)} %copy-done, bf16[768,768]{1,0:T(8,128)(2,1)S(1)} %copy-done.12, bf16[768,768]{1,0:T(8,128)(2,1)S(1)} %copy-done.14, ...), custom_call_target="tpu_custom_call" | custom-call | flops 8999999488 | bytes 10000000 | tf_op jit(solution)/shard_map/attention_1/pallas_call | solution.py:568
  182.4 8.1 %feed_1.1 = f32[2,512,768]{2,1,0:T(8,128)} custom-call(f32[1,512,768]{2,1,0:T(8,128)S(1)} %attention_1.1.attended, f32[1,768]{1,0:T(1,128)S(1)} %copy-done.1, bf16[768,3072]{1,0:T(8,128)(2,1)S(1)} %bitcast.24, bf16[3072,768]{1,0:T(8,128)(2,1)S(1)} %bitcast.28, f32[2,512,768]{2,1,0:T(8,128)} %feed_0.1.held), custom_call_target="tpu_custom_call", output_to_operand_aliasing={{}: (4, {})} | custom-call | flops 6000000000 | bytes 10000000 | tf_op jit(solution)/shard_map/feed_1/pallas_call | solution.py:610
  192.1 2.8 %last.1 = (f32[768,768]{1,0:T(8,128)}, f32[768,768]{1,0:T(8,128)}, f32[8,768]{1,0:T(8,128)S(1)}) custom-call(bf16[32,56,768]{2,1,0:T(8,128)(2,1)S(1)} %constant_dynamic-update-slice_fusion.5.gathered), custom_call_target="tpu_custom_call" | custom-call | flops 10000000 | bytes 10000000 | tf_op jit(solution)/shard_map/last/pallas_call | solution.py:786
  196.2 2.3 %copy-done.5 = bf16[512,4608]{1,0:T(8,128)(2,1)S(1)} copy-done((bf16[512,4608]{1,0:T(8,128)(2,1)S(1)}, bf16[512,4608]{1,0:T(8,128)(2,1)}, u32[]{:S(2)}) %copy-start.5) | copy-done | bytes 4718616
  198.5 19.1 %outer.1 = (f32[768,3072]{1,0:T(8,128)}, f32[3072,768]{1,0:T(8,128)}, f32[768,768]{1,0:T(8,128)}, f32[768,768]{1,0:T(8,128)}) custom-call(bf16[512,4608]{1,0:T(8,128)(2,1)S(1)} %copy-done.5, f32[512,1]{1,0:T(8,128)S(1)} %reshape.113.g, bf16[768,3072]{1,0:T(8,128)(2,1)} %get-tuple-element.55.i.wi, bf16[3072,768]{1,0:T(8,128)(2,1)} %get-tuple-element.56.f.wf), custom_call_target="tpu_custom_call" | custom-call | flops 11000000512 | bytes 40000000 | tf_op jit(solution)/shard_map/outer/pallas_call | solution.py:733
  (143 shorter events, 45.9 us)
Async XLA Ops:
  7.2 189.0 %all-gather.2.cloned.1.call-start = ((), (), s32[]{:S(2)}) async-start(), calls=%async_computation | async-start | bytes 4866048 | tf_op jit(solution)/shard_map/all_gather | solution.py:831
  13.7 45.9 %copy-start.3 = (f32[1,768]{1,0:T(1,128)S(1)}, f32[1,768]{1,0:T(1,128)}, u32[]{:S(2)}) copy-start(f32[1,768]{1,0:T(1,128)} %reshape.107.final_gain) | copy-start | bytes 9220
  13.7 45.9 %copy-start.4 = (f32[1,768]{1,0:T(1,128)S(1)}, f32[1,768]{1,0:T(1,128)}, u32[]{:S(2)}) copy-start(f32[1,768]{1,0:T(1,128)} %reshape.108.score_vector) | copy-start | bytes 9220
  38.5 5.8 %collective-permute-start = (f32[1,128]{1,0:T(1,128)}, f32[1,128]{1,0:T(1,128)S(1)}, u32[]{:S(2)}, u32[]{:S(2)}) collective-permute-start(f32[1,128]{1,0:T(1,128)} %get-tuple-element.57), channel_id=1, source_target_pairs={{0,16},{2,18},{4,20},{6,22},{8,24},{10,26},{12,28},{14,30},{16,0},... | collective-permute-start | bytes 1544 | tf_op jit(solution)/shard_map/ppermute | solution.py:818
  44.9 3.6 %collective-permute-start.1 = (f32[2,128]{1,0:T(2,128)S(1)}, f32[2,128]{1,0:T(2,128)S(1)}, u32[]{:S(2)}, u32[]{:S(2)}) collective-permute-start(f32[2,128]{1,0:T(2,128)S(1)} %pad_maximum_fusion.6), channel_id=1, source_target_pairs={{0,8},{2,10},{4,12},{6,14},{8,0},{10,2},{12,4},{14,6},{16,24},{18,... | collective-permute-start | bytes 3080 | tf_op jit(solution)/shard_map/ppermute | solution.py:818
  49.2 3.6 %collective-permute-start.2 = (f32[4,128]{1,0:T(4,128)S(1)}, f32[4,128]{1,0:T(4,128)S(1)}, u32[]{:S(2)}, u32[]{:S(2)}) collective-permute-start(f32[4,128]{1,0:T(4,128)S(1)} %pad_maximum_fusion.5), channel_id=1, source_target_pairs={{0,4},{2,6},{4,0},{6,2},{8,12},{10,14},{12,8},{14,10},{16,20},{18,... | collective-permute-start | bytes 6152 | tf_op jit(solution)/shard_map/ppermute | solution.py:818
  53.4 3.6 %collective-permute-start.3 = (f32[8,128]{1,0:T(8,128)S(1)}, f32[8,128]{1,0:T(8,128)S(1)}, u32[]{:S(2)}, u32[]{:S(2)}) collective-permute-start(f32[8,128]{1,0:T(8,128)S(1)} %pad_maximum_fusion.4), channel_id=1, source_target_pairs={{0,2},{2,0},{4,6},{6,4},{8,10},{10,8},{12,14},{14,12},{16,18},{18,... | collective-permute-start | bytes 12296 | tf_op jit(solution)/shard_map/ppermute | solution.py:818
  57.7 1.2 collective-permute-start.4
  67.8 2.9 %collective-permute-start.5 = (bf16[16,48,768]{2,1,0:T(8,128)(2,1)S(1)}, bf16[16,48,768]{2,1,0:T(8,128)(2,1)S(1)}, u32[]{:S(2)}, u32[]{:S(2)}) collective-permute-start(bf16[16,48,768]{2,1,0:T(8,128)(2,1)S(1)} %get-tuple-element.74), channel_id=1, source_target_pairs={{0,1},{1,0},{2,3},{3,2},{4,5},{5,4},{6,7},{7,6},{8,9},{9,8},{10,11... | collective-permute-start | bytes 3538952 | tf_op jit(solution)/shard_map/ppermute | solution.py:818
  71.0 32.9 %copy-start.21 = (bf16[192,768]{1,0:T(8,128)(2,1)S(1)}, bf16[192,768]{1,0:T(8,128)(2,1)}, u32[]{:S(2)}) copy-start(bf16[192,768]{1,0:T(8,128)(2,1)} %get-tuple-element.69.yv) | copy-start | bytes 884740
  71.0 32.9 %copy-start.24 = (bf16[192,256]{1,0:T(8,128)(2,1)S(1)}, bf16[192,256]{1,0:T(8,128)(2,1)}, u32[]{:S(2)}) copy-start(bf16[192,256]{1,0:T(8,128)(2,1)} %get-tuple-element.67.dl) | copy-start | bytes 294916
  71.0 32.9 %copy-start.27 = (f32[16,768]{1,0:T(8,128)S(1)}, f32[16,768]{1,0:T(8,128)}, u32[]{:S(2)}) copy-start(f32[16,768]{1,0:T(8,128)} %get-tuple-element.70.yq) | copy-start | bytes 147460
  71.1 15.8 %collective-permute-start.6 = (bf16[8,48,768]{2,1,0:T(8,128)(2,1)S(1)}, bf16[8,48,768]{2,1,0:T(8,128)(2,1)S(1)}, u32[]{:S(2)}, u32[]{:S(2)}) collective-permute-start(bf16[8,48,768]{2,1,0:T(8,128)(2,1)S(1)} %slice.71), channel_id=1, source_target_pairs={{0,2},{2,0},{4,6},{6,4},{8,10},{10,8},{12,14},{14,12},{16,18},{18,... | collective-permute-start | bytes 1769480 | tf_op jit(solution)/shard_map/ppermute | solution.py:818
  73.0 30.9 %copy-start.6 = (f32[1,2,512,768]{3,2,1,0:T(8,128)S(1)}, f32[1,2,512,768]{3,2,1,0:T(8,128)}, u32[]{:S(2)}) copy-start(f32[1,2,512,768]{3,2,1,0:T(8,128)} %param.15) | copy-start | bytes 9437188
  73.0 30.9 %copy-start.8 = (s32[1,2,6]{2,1,0:T(2,128)S(1)}, s32[1,2,6]{2,1,0:T(2,128)}, u32[]{:S(2)}) copy-start(s32[1,2,6]{2,1,0:T(2,128)} %param.16) | copy-start | bytes 148
  73.0 30.9 %copy-start.20 = (bf16[192,768]{1,0:T(8,128)(2,1)S(1)}, bf16[192,768]{1,0:T(8,128)(2,1)}, u32[]{:S(2)}) copy-start(bf16[192,768]{1,0:T(8,128)(2,1)} %get-tuple-element.68.yk) | copy-start | bytes 884740
  87.0 15.3 %collective-permute-start.7 = (bf16[4,48,768]{2,1,0:T(8,128)(2,1)S(1)}, bf16[4,48,768]{2,1,0:T(8,128)(2,1)S(1)}, u32[]{:S(2)}, u32[]{:S(2)}) collective-permute-start(bf16[4,48,768]{2,1,0:T(8,128)(2,1)S(1)} %slice.73), channel_id=1, source_target_pairs={{0,4},{2,6},{4,0},{6,2},{8,12},{10,14},{12,8},{14,10},{16,20},{18,... | collective-permute-start | bytes 884744 | tf_op jit(solution)/shard_map/ppermute | solution.py:818
  102.3 8.6 %collective-permute-start.8 = (bf16[2,48,768]{2,1,0:T(8,128)(2,1)S(1)}, bf16[2,48,768]{2,1,0:T(8,128)(2,1)S(1)}, u32[]{:S(2)}, u32[]{:S(2)}) collective-permute-start(bf16[2,48,768]{2,1,0:T(8,128)(2,1)S(1)} %slice.75), channel_id=1, source_target_pairs={{0,8},{2,10},{4,12},{6,14},{8,0},{10,2},{12,4},{14,6},{16,24},{18,... | collective-permute-start | bytes 442376 | tf_op jit(solution)/shard_map/ppermute | solution.py:818
  111.0 6.5 %collective-permute-start.9 = (bf16[1,48,768]{2,1,0:T(8,128)(2,1)S(1)}, bf16[1,48,768]{2,1,0:T(8,128)(2,1)S(1)}, u32[]{:S(2)}, u32[]{:S(2)}) collective-permute-start(bf16[1,48,768]{2,1,0:T(8,128)(2,1)S(1)} %slice.77), channel_id=1, source_target_pairs={{0,16},{2,18},{4,20},{6,22},{8,24},{10,26},{12,28},{14,30},{16,0},... | collective-permute-start | bytes 221192 | tf_op jit(solution)/shard_map/ppermute | solution.py:818
  118.2 6.3 %collective-permute-start.10 = (bf16[1,56,768]{2,1,0:T(8,128)(2,1)S(1)}, bf16[1,56,768]{2,1,0:T(8,128)(2,1)S(1)}, u32[]{:S(2)}, u32[]{:S(2)}) collective-permute-start(bf16[1,56,768]{2,1,0:T(8,128)(2,1)S(1)} %get-tuple-element.91), channel_id=1, source_target_pairs={{0,16},{2,18},{4,20},{6,22},{8,24},{10,26},{12,28},{14,30},{16,0},... | collective-permute-start | bytes 258056 | tf_op jit(solution)/shard_map/ppermute | solution.py:818
  124.5 5.5 %collective-permute-start.11 = (bf16[2,56,768]{2,1,0:T(8,128)(2,1)S(1)}, bf16[2,56,768]{2,1,0:T(8,128)(2,1)S(1)}, u32[]{:S(2)}, u32[]{:S(2)}) collective-permute-start(bf16[2,56,768]{2,1,0:T(8,128)(2,1)S(1)} %pad_maximum_fusion.2), channel_id=1, source_target_pairs={{0,8},{2,10},{4,12},{6,14},{8,0},{10,2},{12,4},{14,6},{16,24},{18,... | collective-permute-start | bytes 516104 | tf_op jit(solution)/shard_map/ppermute | solution.py:818
  130.0 13.7 %collective-permute-start.12 = (bf16[4,56,768]{2,1,0:T(8,128)(2,1)S(1)}, bf16[4,56,768]{2,1,0:T(8,128)(2,1)S(1)}, u32[]{:S(2)}, u32[]{:S(2)}) collective-permute-start(bf16[4,56,768]{2,1,0:T(8,128)(2,1)S(1)} %pad_maximum_fusion.1), channel_id=1, source_target_pairs={{0,4},{2,6},{4,0},{6,2},{8,12},{10,14},{12,8},{14,10},{16,20},{18,... | collective-permute-start | bytes 1032200 | tf_op jit(solution)/shard_map/ppermute | solution.py:818
  144.7 16.5 %collective-permute-start.13 = (bf16[8,56,768]{2,1,0:T(8,128)(2,1)}, bf16[8,56,768]{2,1,0:T(8,128)(2,1)}, u32[]{:S(2)}, u32[]{:S(2)}) collective-permute-start(bf16[8,56,768]{2,1,0:T(8,128)(2,1)} %pad_maximum_fusion), channel_id=1, source_target_pairs={{0,2},{2,0},{4,6},{6,4},{8,10},{10,8},{12,14},{14,12},{16,18},{18,... | collective-permute-start | bytes 2064392 | tf_op jit(solution)/shard_map/ppermute | solution.py:818
  163.2 27.5 %collective-permute-start.14 = (bf16[16,56,768]{2,1,0:T(8,128)(2,1)}, bf16[16,56,768]{2,1,0:T(8,128)(2,1)}, u32[]{:S(2)}, u32[]{:S(2)}) collective-permute-start(bf16[16,56,768]{2,1,0:T(8,128)(2,1)} %get-tuple-element.92), channel_id=1, source_target_pairs={{0,1},{1,0},{2,3},{3,2},{4,5},{5,4},{6,7},{7,6},{8,9},{9,8},{10,11... | collective-permute-start | bytes 4128776 | tf_op jit(solution)/shard_map/ppermute | solution.py:818
  (33 other events, 424.4 us)
Sparse Core Ops, SparseCore 0:
  38.6 73.6 all-gather.1
